TPU v7x, 32 devices: a whole 2x2x4 slice. The times are simulated.
32 devices in a mesh: lat: 4 (over x, core), lon: 8 (over z, y).
Axes of the slice: x: 2, y: 2, z: 4, core: 2. Of those that a mesh axis runs over, the one named last changes fastest.
Arguments:
- features: bfloat16 [8, 128, 256, 256], P(None, 'lat', 'lon'), may hold values from -16 to 16
- band_points: int32 [128], replicated, may hold values from 64 to 256, as said below
- survival_flags: int32 [8, 2], replicated, may hold values 0 or 1
- first_kernel_weight: bfloat16 [3, 3, 256, 256], replicated, may hold values from -0.125 to 0.125
- second_kernel_weight: bfloat16 [3, 3, 256, 256], replicated, may hold values from -0.125 to 0.125
Outputs:
- section_result: bfloat16 [8, 128, 256, 256], P(None, 'lat', 'lon')
Inputs may be any that keep to these rules, and one draw needn't show every extreme that they name: `band_points`: the live points of a row are its first ones.
All inputs are finite; a program needn't handle non-finite values.
Results may differ from a plain program's by a relative error of at most 0.0006.
The roundings to bfloat16 on the way count: a program that leaves them out, or rounds other values in their place, can miss the bound.
Values may be sent and summed in bfloat16 or wider, within the bound.
A program may use at most 320 MiB of HBM per device.

v0:
```python
import functools

import jax
import jax.numpy as jnp
from jax import lax
from jax.experimental import pallas as pl
from jax.experimental.pallas import tpu as pltpu
from jax.sharding import PartitionSpec as P

GROUPS = 32
DILATIONS = (2, 4)
EPS = 1e-05
KEEP_RATE = 0.8
LANES = 128
ROWS_PER_STEP = 2
MESH = pl.DeviceIdType.MESH
HIGHEST = lax.Precision.HIGHEST


def kernel(
    n_lat, n_lon, tile_rows, tile_cols, samples, channels,
    feat_ref, points_ref, flags_ref, w1_ref, w2_ref, out_ref,
    x_ref, pad1, pad2, mine, lat_slots, lon_slots,
    stat_send, stat_recv, halo_send, halo_recv,
):
    cells = tile_cols * samples
    group_size = channels // GROUPS
    lat = lax.axis_index("lat")
    lon = lax.axis_index("lon")
    row0 = lat * tile_rows
    col0 = lon * tile_cols

    barrier = pltpu.get_barrier_semaphore()
    for k in range(1, n_lat):
        pl.semaphore_signal(
            barrier, inc=1, device_id={"lat": lax.rem(lat + k, n_lat)}, device_id_type=MESH
        )
    for k in range(1, n_lon):
        pl.semaphore_signal(
            barrier, inc=1, device_id={"lon": lax.rem(lon + k, n_lon)}, device_id_type=MESH
        )

    def live(row, first, width):
        column = lax.broadcasted_iota(jnp.int32, (width, channels), 0) // samples
        return column + (first // samples + col0) < points_ref[row0 + row]

    def per_sample(values):
        return values.reshape(-1, samples, channels).sum(axis=0)

    member = (
        lax.broadcasted_iota(jnp.int32, (channels, LANES), 0) // group_size
        == lax.broadcasted_iota(jnp.int32, (channels, LANES), 1)
    ).astype(jnp.float32)
    spread_map = (
        lax.broadcasted_iota(jnp.int32, (LANES, channels), 1) // group_size
        == lax.broadcasted_iota(jnp.int32, (LANES, channels), 0)
    ).astype(jnp.float32)

    def group_total(values):
        return jnp.dot(values, member, precision=HIGHEST, preferred_element_type=jnp.float32)

    def spread(values):
        return jnp.dot(values, spread_map, precision=HIGHEST, preferred_element_type=jnp.float32)

    def count_row(i, total):
        return total + jnp.clip(points_ref[row0 + i] - col0, 0, tile_cols)

    local_cells = lax.fori_loop(0, tile_rows, count_row, jnp.int32(0))
    local_count = jnp.full((samples, LANES), local_cells * group_size, jnp.int32).astype(
        jnp.float32
    )

    def combine(parts):
        total = sum(p[0] for p in parts)
        count = sum(p[2] for p in parts)
        mean = total / jnp.maximum(count, 1.0)
        spreads = None
        for p in parts:
            gap = p[0] / jnp.maximum(p[2], 1.0) - mean
            term = p[1] + p[2] * gap * gap
            spreads = term if spreads is None else spreads + term
        return total, spreads, count, mean

    def exchange(round_index, stage, axis, index, peers, slots):
        copies = []
        base = (round_index * 2 + stage) * max(n_lat, n_lon)
        for k in range(1, peers):
            copy = pltpu.make_async_remote_copy(
                src_ref=mine.at[round_index, stage],
                dst_ref=slots.at[round_index, k],
                send_sem=stat_send.at[base + k],
                recv_sem=stat_recv.at[base + k],
                device_id={axis: lax.rem(index + k, peers)},
                device_id_type=MESH,
            )
            copy.start()
            copies.append(copy)
        for copy in copies:
            copy.wait()
        parts = [tuple(mine[round_index, stage, j] for j in range(3))]
        for k in range(1, peers):
            parts.append(tuple(slots[round_index, k, j] for j in range(3)))
        return combine(parts)

    def sum_row(i, total):
        values = x_ref[i].astype(jnp.float32)
        return total + per_sample(jnp.where(live(i, 0, cells), values, 0.0))

    def load_row(i, total):
        values = jnp.swapaxes(feat_ref[:, i].astype(jnp.float32), 0, 1)
        values = values.reshape(cells, channels)
        x_ref[i] = values.astype(jnp.bfloat16)
        return total + per_sample(jnp.where(live(i, 0, cells), values, 0.0))

    def local_statistics(round_index, row_body):
        zero = jnp.zeros((samples, channels), jnp.float32)
        total = group_total(lax.fori_loop(0, tile_rows, row_body, zero))
        mean = spread(total / jnp.maximum(local_count, 1.0))

        def square_row(i, acc):
            values = x_ref[i].astype(jnp.float32).reshape(tile_cols, samples, channels)
            gap = (values - mean[None]).reshape(cells, channels)
            return acc + per_sample(jnp.where(live(i, 0, cells), gap * gap, 0.0))

        squares = group_total(lax.fori_loop(0, tile_rows, square_row, zero))
        mine[round_index, 0, 0] = total
        mine[round_index, 0, 1] = squares
        mine[round_index, 0, 2] = local_count

    def global_statistics(round_index):
        total, squares, count, _ = exchange(round_index, 0, "lat", lat, n_lat, lat_slots)
        mine[round_index, 1, 0] = total
        mine[round_index, 1, 1] = squares
        mine[round_index, 1, 2] = count
        total, squares, count, mean = exchange(round_index, 1, "lon", lon, n_lon, lon_slots)
        inv_std = lax.rsqrt(squares / jnp.maximum(count, 1.0) + EPS)
        return spread(mean), spread(inv_std) * 0.5

    def block(round_index, pad, w_ref, mean, half_scale):
        d = DILATIONS[round_index]
        side = d * samples
        rows = tile_rows

        def act(i, first, width):
            values = x_ref[i, pl.ds(first, width), :].astype(jnp.float32)
            values = values.reshape(width // samples, samples, channels)
            half = ((values - mean[None]) * half_scale[None]).reshape(width, channels)
            hidden = half * jnp.tanh(half) + half
            hidden = jnp.where(live(i, first, width), hidden, 0.0)
            pad[d + i, pl.ds(side + first, width), :] = hidden.astype(jnp.bfloat16)

        def remote(number, src, dst, target):
            return pltpu.make_async_remote_copy(
                src_ref=src,
                dst_ref=dst,
                send_sem=halo_send.at[round_index * 8 + number],
                recv_sem=halo_recv.at[round_index * 8 + number],
                device_id=target,
                device_id_type=MESH,
            )

        middle = pl.ds(side, cells)
        up = {"lat": lax.rem(lat + n_lat - 1, n_lat)}
        down = {"lat": lax.rem(lat + 1, n_lat)}
        right = {"lon": lax.rem(lon + 1, n_lon)}
        left = {"lon": lax.rem(lon + n_lon - 1, n_lon)}
        to_up = remote(0, pad.at[pl.ds(d, d), middle], pad.at[pl.ds(d + rows, d), middle], up)
        to_down = remote(1, pad.at[pl.ds(rows, d), middle], pad.at[pl.ds(0, d), middle], down)

        def sideways(number, first, height):
            span = pl.ds(first, height)
            return [
                remote(
                    number, pad.at[span, pl.ds(cells, side)], pad.at[span, pl.ds(0, side)], right
                ),
                remote(
                    number + 1,
                    pad.at[span, pl.ds(side, side)],
                    pad.at[span, pl.ds(side + cells, side)],
                    left,
                ),
            ]

        flanks = sideways(2, d, rows)
        corners = sideways(4, 0, d) + sideways(6, d + rows, d)

        @pl.loop(0, d)
        def _(i):
            act(i, 0, cells)
            act(rows - d + i, 0, cells)

        @pl.when(lat > 0)
        def _():
            to_up.start()

        @pl.when(lat < n_lat - 1)
        def _():
            to_down.start()

        @pl.loop(d, rows - d)
        def _(i):
            act(i, 0, side)
            act(i, cells - side, side)

        for copy in flanks:
            copy.start()

        @pl.loop(d, rows - d)
        def _(i):
            act(i, side, cells - 2 * side)

        @pl.when(lat == 0)
        def _():
            pad[pl.ds(0, d), middle, :] = jnp.zeros((d, cells, channels), jnp.bfloat16)

        @pl.when(lat == n_lat - 1)
        def _():
            pad[pl.ds(d + rows, d), middle, :] = jnp.zeros((d, cells, channels), jnp.bfloat16)

        @pl.when(lat > 0)
        def _():
            to_down.wait_recv()
            to_up.wait_send()

        @pl.when(lat < n_lat - 1)
        def _():
            to_up.wait_recv()
            to_down.wait_send()

        for copy in corners:
            copy.start()

        sample_index = lax.broadcasted_iota(jnp.int32, (samples, channels), 0)
        flag = jnp.zeros((samples, channels), jnp.int32)
        for s in range(samples):
            flag = jnp.where(sample_index == s, flags_ref[s, round_index], flag)
        kept = flag.astype(jnp.float32) / KEEP_RATE

        def conv(first_row, height, first, width):
            taps = [
                pad[
                    pl.ds(first_row + r * d, height), pl.ds(first + c * side, width), :
                ].reshape(height * width, channels)
                for r in range(3)
                for c in range(3)
            ]
            summed = jnp.dot(
                jnp.concatenate(taps, axis=1), w_ref[...], preferred_element_type=jnp.float32
            )
            summed = summed.reshape(height * width // samples, samples, channels) * kept[None]
            where = (pl.ds(first_row, height), pl.ds(first, width), slice(None))
            old = x_ref[where].astype(jnp.float32)
            x_ref[where] = (old + summed.reshape(height, width, channels)).astype(jnp.bfloat16)

        @pl.loop(0, tile_rows // ROWS_PER_STEP)
        def _(step):
            conv(step * ROWS_PER_STEP, ROWS_PER_STEP, side, cells - 2 * side)

        for copy in flanks + corners:
            copy.wait()

        strip_rows = 512 // side

        @pl.loop(0, tile_rows // strip_rows)
        def _(step):
            conv(step * strip_rows, strip_rows, 0, side)
            conv(step * strip_rows, strip_rows, cells - side, side)

    local_statistics(0, load_row)
    pl.semaphore_wait(barrier, n_lat - 1 + n_lon - 1)
    block(0, pad1, w1_ref, *global_statistics(0))
    local_statistics(1, sum_row)
    block(1, pad2, w2_ref, *global_statistics(1))

    @pl.loop(0, tile_rows)
    def _(i):
        values = x_ref[i].astype(jnp.float32).reshape(tile_cols, samples, channels)
        out_ref[:, i] = jnp.swapaxes(values, 0, 1).astype(jnp.bfloat16)


def per_device(n_lat, n_lon, features, band_points, survival_flags, first_weight, second_weight):
    samples, rows, cols, channels = features.shape
    d1, d2 = DILATIONS
    vmem = pl.BlockSpec(memory_space=pltpu.VMEM)
    smem = pl.BlockSpec(memory_space=pltpu.SMEM)
    message = (3, samples, LANES)
    slots = 4 * max(n_lat, n_lon)
    taps = (9 * channels, channels)

    def padded(d):
        shape = (rows + 2 * d, (cols + 2 * d) * samples, channels)
        return pltpu.VMEM(shape, jnp.bfloat16)

    return pl.pallas_call(
        functools.partial(kernel, n_lat, n_lon, rows, cols, samples, channels),
        out_shape=jax.ShapeDtypeStruct(features.shape, jnp.bfloat16),
        in_specs=[vmem, smem, smem, vmem, vmem],
        out_specs=vmem,
        scratch_shapes=[
            pltpu.VMEM((rows, cols * samples, channels), jnp.bfloat16),
            padded(d1),
            padded(d2),
            pltpu.VMEM((2, 2) + message, jnp.float32),
            pltpu.VMEM((2, n_lat) + message, jnp.float32),
            pltpu.VMEM((2, n_lon) + message, jnp.float32),
            pltpu.SemaphoreType.DMA((slots,)),
            pltpu.SemaphoreType.DMA((slots,)),
            pltpu.SemaphoreType.DMA((16,)),
            pltpu.SemaphoreType.DMA((16,)),
        ],
        compiler_params=pltpu.CompilerParams(
            collective_id=0, has_side_effects=True, vmem_limit_bytes=56 * 2**20
        ),
    )(
        features,
        band_points,
        survival_flags,
        first_weight.reshape(taps),
        second_weight.reshape(taps),
    )


def solution(mesh):
    in_specs = (P(None, "lat", "lon", None), P(), P(), P(), P())
    out_specs = P(None, "lat", "lon", None)
    return jax.shard_map(
        functools.partial(per_device, mesh.shape["lat"], mesh.shape["lon"]),
        mesh=mesh,
        in_specs=in_specs,
        out_specs=out_specs,
        check_vma=False,
    )
```

profile of v0, /device:TPU:0, one launch (start us, length us, event | category | flops | bytes accessed | tf_op | source)
XLA Modules:
  0.0 91.3 jit_solution(2040957939328189821)
XLA Ops:
  0.0 1.3 %copy.6.flags_ref = s32[8,2]{1,0:T(8,128)} copy(s32[8,2]{0,1:T(2,128)} %param.7) | data formatting | bytes 128 | tf_op args[2]
  1.3 85.3 %shard_map.55 = bf16[8,32,32,256]{3,2,1,0:T(8,128)(2,1)} custom-call(bf16[8,32,32,256]{3,2,1,0:T(8,128)(2,1)} %feat_ref.1, s32[128]{0:T(128)} %points_ref.1, s32[8,2]{1,0:T(8,128)} %copy.6.flags_ref, bf16[2304,256]{1,0:T(8,128)(2,1)} %bitcast.2, bf16[2304,256]{1,0:T(8,128)(2,1)} %bitcast.3), custom_call_target="tpu_custom_call" | custom-call | tf_op jit(solution)/shard_map/pallas_call | solution.py:294
  86.7 4.6 %copy.8 = bf16[8,32,32,256]{3,2,1,0:T(8,128)(2,1)} copy(bf16[8,32,32,256]{3,2,1,0:T(8,128)(2,1)} %shard_map.55) | data formatting | bytes 8388608
where the time goes:
time: 91.5 us; the launch traced here: 91.3 us
  Pallas kernels  85.3 us (93%)
  local copies, waits for them, and re-layouts  5.99 us (7%)
    pallas_call x1, Pallas kernels, per_device(): pl.pallas_call(functools.partial(kernel, n_lat, n_lon, rows, cols, sample...  85.3 us
    unnamed x2, local copies, waits for them, and re-layouts  5.99 us

commit v1 on v0

v1 whole, which is shorter than its diff:
```python
import functools

import jax
import jax.numpy as jnp
from jax import lax
from jax.experimental import pallas as pl
from jax.experimental.pallas import tpu as pltpu
from jax.sharding import PartitionSpec as P

GROUPS = 32
DILATIONS = (2, 4)
EPS = 1e-05
KEEP_RATE = 0.8
LANES = 128
ROWS_PER_STEP = 4
LOAD_CHUNKS = 4
MESH = pl.DeviceIdType.MESH


def kernel(
    n_lat, n_lon, tile_rows, tile_cols, samples, channels,
    feat_hbm, points_ref, flags_ref, w1_hbm, w2_hbm, x_ref,
    feat_ref, w1_ref, w2_ref, pad1, pad2, total_ref, mine, lat_slots, lon_slots,
    local_sem, stat_send, stat_recv, halo_send, halo_recv,
):
    cells = tile_cols * samples
    group_size = channels // GROUPS
    lat = lax.axis_index("lat")
    lon = lax.axis_index("lon")
    row0 = lat * tile_rows
    col0 = lon * tile_cols

    chunk = tile_rows // LOAD_CHUNKS
    loads = []
    for c in range(LOAD_CHUNKS):
        part = (slice(None), pl.ds(c * chunk, chunk))
        loads.append((feat_hbm.at[part], feat_ref.at[part]))
    loads += [(w1_hbm, w1_ref), (w2_hbm, w2_ref)]
    loads = [pltpu.make_async_copy(*ends, local_sem.at[k]) for k, ends in enumerate(loads)]
    for copy in loads:
        copy.start()

    barrier = pltpu.get_barrier_semaphore()
    for k in range(1, n_lat):
        pl.semaphore_signal(
            barrier, inc=1, device_id={"lat": lax.rem(lat + k, n_lat)}, device_id_type=MESH
        )
    for k in range(1, n_lon):
        pl.semaphore_signal(
            barrier, inc=1, device_id={"lon": lax.rem(lon + k, n_lon)}, device_id_type=MESH
        )

    def live(row, first, width):
        shape = (width // samples, samples, channels)
        column = lax.broadcasted_iota(jnp.int32, shape, 0)
        return column + (first // samples + col0) < points_ref[row0 + row]

    def cubed(values):
        return values.reshape(-1, samples, channels)

    halves = channels // LANES

    def pack(values):
        return jnp.concatenate(jnp.split(values, halves, axis=1), axis=0)

    def unpack(values):
        return jnp.concatenate(jnp.split(values, halves, axis=0), axis=1)

    lane = lax.broadcasted_iota(jnp.int32, (halves * samples, LANES), 1)
    place = lane % group_size

    def group_total(values):
        step = 1
        while step < group_size:
            above = pltpu.roll(values, LANES - step, 1)
            below = pltpu.roll(values, step, 1)
            values = values + jnp.where((lane & step) == 0, above, below)
            step *= 2
        return values

    def spread(values):
        return unpack(group_total(jnp.where(place == 0, values, 0.0)))

    def message(total, squares, count):
        return jnp.where(place == 0, total, jnp.where(place == 1, squares, count))

    def count_row(i, total):
        return total + jnp.clip(points_ref[row0 + i] - col0, 0, tile_cols)

    local_cells = lax.fori_loop(0, tile_rows, count_row, jnp.int32(0))
    local_count = jnp.full((halves * samples, LANES), local_cells * group_size, jnp.int32).astype(
        jnp.float32
    )

    def combine(parts):
        total = sum(p[0] for p in parts)
        count = sum(p[2] for p in parts)
        mean = total / jnp.maximum(count, 1.0)
        spreads = None
        for p in parts:
            gap = p[0] / jnp.maximum(p[2], 1.0) - mean
            term = p[1] + p[2] * gap * gap
            spreads = term if spreads is None else spreads + term
        return total, spreads, count, mean

    def exchange(round_index, stage, axis, index, peers, slots):
        copies = []
        base = (round_index * 2 + stage) * max(n_lat, n_lon)
        for k in range(1, peers):
            copy = pltpu.make_async_remote_copy(
                src_ref=mine.at[round_index, stage],
                dst_ref=slots.at[round_index, k],
                send_sem=stat_send.at[base + k],
                recv_sem=stat_recv.at[base + k],
                device_id={axis: lax.rem(index + k, peers)},
                device_id_type=MESH,
            )
            copy.start()
            copies.append(copy)
        for copy in copies:
            copy.wait()
        packed = [mine[round_index, stage]] + [slots[round_index, k] for k in range(1, peers)]
        return combine(
            [(p, pltpu.roll(p, LANES - 1, 1), pltpu.roll(p, LANES - 2, 1)) for p in packed]
        )

    def load_row(i, total):
        values = jnp.swapaxes(feat_ref[:, i].astype(jnp.float32), 0, 1)
        x_ref[i] = values.reshape(cells, channels).astype(jnp.bfloat16)
        return total + jnp.where(live(i, 0, cells), values, 0.0).sum(axis=0)

    def local_statistics(round_index, channel_total):
        total = group_total(pack(channel_total))
        mean = unpack(total / jnp.maximum(local_count, 1.0))

        def square_row(i, acc):
            gap = cubed(x_ref[i].astype(jnp.float32)) - mean[None]
            return acc + jnp.where(live(i, 0, cells), gap * gap, 0.0).sum(axis=0)

        zero = jnp.zeros((samples, channels), jnp.float32)
        squares = group_total(pack(lax.fori_loop(0, tile_rows, square_row, zero)))
        mine[round_index, 0] = message(total, squares, local_count)

    def global_statistics(round_index):
        total, squares, count, _ = exchange(round_index, 0, "lat", lat, n_lat, lat_slots)
        mine[round_index, 1] = message(
            total, pltpu.roll(squares, 1, 1), pltpu.roll(count, 2, 1)
        )
        total, squares, count, mean = exchange(round_index, 1, "lon", lon, n_lon, lon_slots)
        inv_std = lax.rsqrt(squares / jnp.maximum(count, 1.0) + EPS)
        return spread(mean), spread(inv_std) * 0.5

    def block(round_index, pad, w_ref, weight_load, mean, half_scale):
        d = DILATIONS[round_index]
        side = d * samples
        rows = tile_rows

        def act(i, first, width):
            values = cubed(x_ref[i, pl.ds(first, width), :].astype(jnp.float32))
            half = (values - mean[None]) * half_scale[None]
            hidden = half * jnp.tanh(half) + half
            hidden = jnp.where(live(i, first, width), hidden, 0.0).reshape(width, channels)
            pad[d + i, pl.ds(side + first, width), :] = hidden.astype(jnp.bfloat16)

        def remote(number, src, dst, target):
            return pltpu.make_async_remote_copy(
                src_ref=src,
                dst_ref=dst,
                send_sem=halo_send.at[round_index * 8 + number],
                recv_sem=halo_recv.at[round_index * 8 + number],
                device_id=target,
                device_id_type=MESH,
            )

        middle = pl.ds(side, cells)
        up = {"lat": lax.rem(lat + n_lat - 1, n_lat)}
        down = {"lat": lax.rem(lat + 1, n_lat)}
        right = {"lon": lax.rem(lon + 1, n_lon)}
        left = {"lon": lax.rem(lon + n_lon - 1, n_lon)}
        to_up = remote(0, pad.at[pl.ds(d, d), middle], pad.at[pl.ds(d + rows, d), middle], up)
        to_down = remote(1, pad.at[pl.ds(rows, d), middle], pad.at[pl.ds(0, d), middle], down)

        def sideways(number, first, height):
            span = pl.ds(first, height)
            return [
                remote(
                    number, pad.at[span, pl.ds(cells, side)], pad.at[span, pl.ds(0, side)], right
                ),
                remote(
                    number + 1,
                    pad.at[span, pl.ds(side, side)],
                    pad.at[span, pl.ds(side + cells, side)],
                    left,
                ),
            ]

        flanks = sideways(2, d, rows)
        corners = sideways(4, 0, d) + sideways(6, d + rows, d)

        @pl.loop(0, d)
        def _(i):
            act(i, 0, cells)
            act(rows - d + i, 0, cells)

        @pl.when(lat > 0)
        def _():
            to_up.start()

        @pl.when(lat < n_lat - 1)
        def _():
            to_down.start()

        @pl.loop(d, rows - d)
        def _(i):
            act(i, 0, side)
            act(i, cells - side, side)

        for copy in flanks:
            copy.start()

        @pl.loop(d, rows - d)
        def _(i):
            act(i, side, cells - 2 * side)

        @pl.when(lat == 0)
        def _():
            pad[pl.ds(0, d), middle, :] = jnp.zeros((d, cells, channels), jnp.bfloat16)

        @pl.when(lat == n_lat - 1)
        def _():
            pad[pl.ds(d + rows, d), middle, :] = jnp.zeros((d, cells, channels), jnp.bfloat16)

        flag = jnp.broadcast_to(flags_ref[:, round_index : round_index + 1], (samples, channels))
        kept = flag.astype(jnp.float32) / KEEP_RATE
        weight_load.wait()

        def conv(first_row, height, first, width):
            taps = [
                pad[
                    pl.ds(first_row + r * d, height), pl.ds(first + c * side, width), :
                ].reshape(height * width, channels)
                for r in range(3)
                for c in range(3)
            ]
            summed = jnp.dot(
                jnp.concatenate(taps, axis=1), w_ref[...], preferred_element_type=jnp.float32
            )
            summed = (cubed(summed) * kept[None]).reshape(height, width, channels)
            where = (pl.ds(first_row, height), pl.ds(first, width), slice(None))
            new = (x_ref[where].astype(jnp.float32) + summed).astype(jnp.bfloat16)
            x_ref[where] = new
            if round_index == 0:
                total = total_ref[...]
                for k in range(height):
                    values = cubed(new[k].astype(jnp.float32))
                    mask = live(first_row + k, first, width)
                    total = total + jnp.where(mask, values, 0.0).sum(axis=0)
                total_ref[...] = total

        def inner(step):
            conv(step * ROWS_PER_STEP, ROWS_PER_STEP, side, cells - 2 * side)

        steps = tile_rows // ROWS_PER_STEP
        pl.loop(1, steps // 2)(inner)

        @pl.when(lat > 0)
        def _():
            to_down.wait_recv()
            to_up.wait_send()

        @pl.when(lat < n_lat - 1)
        def _():
            to_up.wait_recv()
            to_down.wait_send()

        for copy in corners:
            copy.start()

        pl.loop(steps // 2, steps - 1)(inner)
        pl.loop(0, 2)(lambda k: inner(k * (steps - 1)))

        for copy in flanks + corners:
            copy.wait()

        strip_rows = 512 // side

        @pl.loop(0, tile_rows // strip_rows)
        def _(step):
            conv(step * strip_rows, strip_rows, 0, side)
            conv(step * strip_rows, strip_rows, cells - side, side)

    total = jnp.zeros((samples, channels), jnp.float32)
    total_ref[...] = total
    for c in range(LOAD_CHUNKS):
        loads[c].wait()
        total = lax.fori_loop(c * chunk, (c + 1) * chunk, load_row, total)
    local_statistics(0, total)
    pl.semaphore_wait(barrier, n_lat - 1 + n_lon - 1)
    block(0, pad1, w1_ref, loads[LOAD_CHUNKS], *global_statistics(0))
    local_statistics(1, total_ref[...])
    block(1, pad2, w2_ref, loads[LOAD_CHUNKS + 1], *global_statistics(1))


def reorder(x_ref, out_ref):
    samples, rows, cols, channels = out_ref.shape
    for i in range(rows):
        values = x_ref[i].astype(jnp.float32).reshape(cols, samples, channels)
        out_ref[:, i] = jnp.swapaxes(values, 0, 1).astype(jnp.bfloat16)


def per_device(n_lat, n_lon, features, band_points, survival_flags, first_weight, second_weight):
    samples, rows, cols, channels = features.shape
    d1, d2 = DILATIONS
    vmem = pl.BlockSpec(memory_space=pltpu.VMEM)
    smem = pl.BlockSpec(memory_space=pltpu.SMEM)
    message = (samples * channels // LANES, LANES)
    anywhere = pl.BlockSpec(memory_space=pl.ANY)
    slots = 4 * max(n_lat, n_lon)
    taps = (9 * channels, channels)

    def padded(d):
        shape = (rows + 2 * d, (cols + 2 * d) * samples, channels)
        return pltpu.VMEM(shape, jnp.bfloat16)

    ordered = pl.pallas_call(
        functools.partial(kernel, n_lat, n_lon, rows, cols, samples, channels),
        out_shape=jax.ShapeDtypeStruct((rows, cols * samples, channels), jnp.bfloat16),
        in_specs=[anywhere, smem, vmem, anywhere, anywhere],
        out_specs=vmem,
        scratch_shapes=[
            pltpu.VMEM(features.shape, jnp.bfloat16),
            pltpu.VMEM(taps, jnp.bfloat16),
            pltpu.VMEM(taps, jnp.bfloat16),
            padded(d1),
            padded(d2),
            pltpu.VMEM((samples, channels), jnp.float32),
            pltpu.VMEM((2, 2) + message, jnp.float32),
            pltpu.VMEM((2, n_lat) + message, jnp.float32),
            pltpu.VMEM((2, n_lon) + message, jnp.float32),
            pltpu.SemaphoreType.DMA((LOAD_CHUNKS + 2,)),
            pltpu.SemaphoreType.DMA((slots,)),
            pltpu.SemaphoreType.DMA((slots,)),
            pltpu.SemaphoreType.DMA((16,)),
            pltpu.SemaphoreType.DMA((16,)),
        ],
        compiler_params=pltpu.CompilerParams(
            collective_id=0, has_side_effects=True, vmem_limit_bytes=56 * 2**20
        ),
    )(
        features,
        band_points,
        survival_flags,
        first_weight.reshape(taps),
        second_weight.reshape(taps),
    )
    return pl.pallas_call(
        reorder,
        grid=(rows // ROWS_PER_STEP,),
        out_shape=jax.ShapeDtypeStruct(features.shape, jnp.bfloat16),
        in_specs=[pl.BlockSpec((ROWS_PER_STEP, cols * samples, channels), lambda i: (i, 0, 0))],
        out_specs=pl.BlockSpec((samples, ROWS_PER_STEP, cols, channels), lambda i: (0, i, 0, 0)),
    )(ordered)


def solution(mesh):
    in_specs = (P(None, "lat", "lon", None), P(), P(), P(), P())
    out_specs = P(None, "lat", "lon", None)
    return jax.shard_map(
        functools.partial(per_device, mesh.shape["lat"], mesh.shape["lon"]),
        mesh=mesh,
        in_specs=in_specs,
        out_specs=out_specs,
        check_vma=False,
    )
```

time: 91.5 us -> 87.5 us (0.956)
  local copies, waits for them, and re-layouts: 5.99 us -> 1.34 us
    pallas_call x0 -> x1, Pallas kernels: none -> 7.44 us  [per_device(): pl.pallas_call(reorder, grid=(rows // ROWS_PER_STEP,), out_shape=jax.Shap...]
    pallas_call x1, Pallas kernels: 85.3 us -> 78.4 us  [per_device(): pl.pallas_call(functools.partial(kernel, n_lat, n_lon, rows, cols, sample...]
    unnamed x2 -> x1, local copies, waits for them, and re-layouts: 5.99 us -> 1.34 us
where the time goes in v1:
time: 87.5 us; the launch traced here: 87.2 us
  Pallas kernels  85.8 us (98%)
  local copies, waits for them, and re-layouts  1.34 us (2%)
    pallas_call x1, Pallas kernels, per_device(): pl.pallas_call(functools.partial(kernel, n_lat, n_lon, rows, cols, sample...  78.4 us
    pallas_call x1, Pallas kernels, per_device(): pl.pallas_call(reorder, grid=(rows // ROWS_PER_STEP,), out_shape=jax.Shap...  7.44 us

profile of v1, /device:TPU:0, one launch (start us, length us, event | category | flops | bytes accessed | tf_op | source)
XLA Modules:
  0.0 87.2 jit_solution(2221671990674699863)
XLA Ops:
  0.0 1.3 %copy.6.flags_ref = s32[8,2]{1,0:T(8,128)} copy(s32[8,2]{0,1:T(2,128)} %param.7) | data formatting | bytes 128 | tf_op args[2]
  1.3 78.4 %shard_map.55.x_ref = bf16[32,256,256]{2,1,0:T(8,128)(2,1)} custom-call(bf16[8,32,32,256]{3,2,1,0:T(8,128)(2,1)} %feat_hbm.1, s32[128]{0:T(128)} %points_ref.1, s32[8,2]{1,0:T(8,128)} %copy.6.flags_ref, bf16[2304,256]{1,0:T(8,128)(2,1)} %bitcast.2, bf16[2304,256]{1,0:T(8,128)(2,1)} %bitcast.3), custom_call_target="tpu_custom_call" | custom-call | tf_op jit(solution)/shard_map/pallas_call | solution.py:325
  79.8 7.4 %shard_map.56 = bf16[8,32,32,256]{3,2,1,0:T(8,128)(2,1)} custom-call(bf16[32,256,256]{2,1,0:T(8,128)(2,1)} %shard_map.55.x_ref), custom_call_target="tpu_custom_call" | custom-call | tf_op jit(solution)/shard_map/pallas_call | solution.py:356

commit v2 on v1

--- a/solution.py
+++ b/solution.py
@@ -12,9 +12,17 @@
 EPS = 1e-05
 KEEP_RATE = 0.8
 LANES = 128
-ROWS_PER_STEP = 4
 LOAD_CHUNKS = 4
+REORDER_ROWS = 8
 MESH = pl.DeviceIdType.MESH
+
+
+def permutation(outer, inner, dtype):
+    size = outer * inner
+    row = lax.broadcasted_iota(jnp.int32, (size, size), 0)
+    col = lax.broadcasted_iota(jnp.int32, (size, size), 1)
+    wanted = lax.rem(row, inner) * outer + row // inner
+    return (col == wanted).astype(jnp.float32).astype(dtype)
 
 
 def kernel(
@@ -50,10 +58,16 @@
             barrier, inc=1, device_id={"lon": lax.rem(lon + k, n_lon)}, device_id_type=MESH
         )
 
+    lat_total = tile_rows * n_lat
+    lon_total = tile_cols * n_lon
+
     def live(row, first, width):
         shape = (width // samples, samples, channels)
-        column = lax.broadcasted_iota(jnp.int32, shape, 0)
-        return column + (first // samples + col0) < points_ref[row0 + row]
+        start = lax.rem(col0 + first // samples + lon_total, lon_total)
+        place = row0 + row
+        points = points_ref[jnp.clip(place, 0, lat_total - 1)]
+        points = jnp.where((place >= 0) & (place < lat_total), points, 0)
+        return lax.broadcasted_iota(jnp.int32, shape, 0) + start < points
 
     def cubed(values):
         return values.reshape(-1, samples, channels)
@@ -124,10 +138,13 @@
             [(p, pltpu.roll(p, LANES - 1, 1), pltpu.roll(p, LANES - 2, 1)) for p in packed]
         )
 
+    by_column = permutation(tile_cols, samples, jnp.bfloat16)
+
     def load_row(i, total):
-        values = jnp.swapaxes(feat_ref[:, i].astype(jnp.float32), 0, 1)
-        x_ref[i] = values.reshape(cells, channels).astype(jnp.bfloat16)
-        return total + jnp.where(live(i, 0, cells), values, 0.0).sum(axis=0)
+        values = feat_ref[:, i].reshape(cells, channels)
+        values = jnp.dot(by_column, values, preferred_element_type=jnp.float32)
+        x_ref[i] = values.astype(jnp.bfloat16)
+        return total + jnp.where(live(i, 0, cells), cubed(values), 0.0).sum(axis=0)
 
     def local_statistics(round_index, channel_total):
         total = group_total(pack(channel_total))
@@ -150,17 +167,18 @@
         inv_std = lax.rsqrt(squares / jnp.maximum(count, 1.0) + EPS)
         return spread(mean), spread(inv_std) * 0.5
 
-    def block(round_index, pad, w_ref, weight_load, mean, half_scale):
+    pads = (pad1, pad2)
+    up = {"lat": lax.rem(lat + n_lat - 1, n_lat)}
+    down = {"lat": lax.rem(lat + 1, n_lat)}
+    right = {"lon": lax.rem(lon + 1, n_lon)}
+    left = {"lon": lax.rem(lon + n_lon - 1, n_lon)}
+
+    def halo_copies(round_index):
         d = DILATIONS[round_index]
         side = d * samples
         rows = tile_rows
-
-        def act(i, first, width):
-            values = cubed(x_ref[i, pl.ds(first, width), :].astype(jnp.float32))
-            half = (values - mean[None]) * half_scale[None]
-            hidden = half * jnp.tanh(half) + half
-            hidden = jnp.where(live(i, first, width), hidden, 0.0).reshape(width, channels)
-            pad[d + i, pl.ds(side + first, width), :] = hidden.astype(jnp.bfloat16)
+        pad = pads[round_index]
+        centre = pl.ds(side, cells)
 
         def remote(number, src, dst, target):
             return pltpu.make_async_remote_copy(
@@ -172,17 +190,21 @@
                 device_id_type=MESH,
             )
 
-        middle = pl.ds(side, cells)
-        up = {"lat": lax.rem(lat + n_lat - 1, n_lat)}
-        down = {"lat": lax.rem(lat + 1, n_lat)}
-        right = {"lon": lax.rem(lon + 1, n_lon)}
-        left = {"lon": lax.rem(lon + n_lon - 1, n_lon)}
-        to_up = remote(0, pad.at[pl.ds(d, d), middle], pad.at[pl.ds(d + rows, d), middle], up)
-        to_down = remote(1, pad.at[pl.ds(rows, d), middle], pad.at[pl.ds(0, d), middle], down)
-
-        def sideways(number, first, height):
-            span = pl.ds(first, height)
-            return [
+        to_up = remote(0, x_ref.at[pl.ds(0, d)], pad.at[pl.ds(d + rows, d), centre], up)
+        to_down = remote(1, x_ref.at[pl.ds(rows - d, d)], pad.at[pl.ds(0, d), centre], down)
+        inner = pl.ds(d, rows)
+        flanks = [
+            remote(
+                2, x_ref.at[:, pl.ds(cells - side, side)], pad.at[inner, pl.ds(0, side)], right
+            ),
+            remote(
+                3, x_ref.at[:, pl.ds(0, side)], pad.at[inner, pl.ds(side + cells, side)], left
+            ),
+        ]
+        corners = []
+        for number, first in ((4, 0), (6, d + rows)):
+            span = pl.ds(first, d)
+            corners += [
                 remote(
                     number, pad.at[span, pl.ds(cells, side)], pad.at[span, pl.ds(0, side)], right
                 ),
@@ -193,46 +215,77 @@
                     left,
                 ),
             ]
-
-        flanks = sideways(2, d, rows)
-        corners = sideways(4, 0, d) + sideways(6, d + rows, d)
-
-        @pl.loop(0, d)
-        def _(i):
-            act(i, 0, cells)
-            act(rows - d + i, 0, cells)
-
-        @pl.when(lat > 0)
-        def _():
-            to_up.start()
-
-        @pl.when(lat < n_lat - 1)
-        def _():
-            to_down.start()
-
-        @pl.loop(d, rows - d)
-        def _(i):
-            act(i, 0, side)
-            act(i, cells - side, side)
-
+        return to_up, to_down, flanks, corners
+
+    def send_halos(round_index):
+        to_up, to_down, flanks, _ = halo_copies(round_index)
         for copy in flanks:
             copy.start()
 
-        @pl.loop(d, rows - d)
-        def _(i):
-            act(i, side, cells - 2 * side)
+        @pl.when(lat > 0)
+        def _():
+            to_up.start()
+
+        @pl.when(lat < n_lat - 1)
+        def _():
+            to_down.start()
+
+    def send_corners(round_index):
+        to_up, to_down, _, corners = halo_copies(round_index)
+        d = DILATIONS[round_index]
+        pad = pads[round_index]
+        centre = pl.ds(d * samples, cells)
+        blank = jnp.zeros((d, cells, channels), jnp.bfloat16)
 
         @pl.when(lat == 0)
         def _():
-            pad[pl.ds(0, d), middle, :] = jnp.zeros((d, cells, channels), jnp.bfloat16)
+            pad[pl.ds(0, d), centre, :] = blank
 
         @pl.when(lat == n_lat - 1)
         def _():
-            pad[pl.ds(d + rows, d), middle, :] = jnp.zeros((d, cells, channels), jnp.bfloat16)
-
-        flag = jnp.broadcast_to(flags_ref[:, round_index : round_index + 1], (samples, channels))
-        kept = flag.astype(jnp.float32) / KEEP_RATE
-        weight_load.wait()
+            pad[pl.ds(d + tile_rows, d), centre, :] = blank
+
+        @pl.when(lat > 0)
+        def _():
+            to_down.wait_recv()
+            to_up.wait_send()
+
+        @pl.when(lat < n_lat - 1)
+        def _():
+            to_up.wait_recv()
+            to_down.wait_send()
+
+        for copy in corners:
+            copy.start()
+
+    def wait_halos(round_index):
+        _, _, flanks, corners = halo_copies(round_index)
+        for copy in flanks + corners:
+            copy.wait()
+
+    def block(round_index, w_ref, weight_load, ahead, mean, half_scale):
+        d = DILATIONS[round_index]
+        side = d * samples
+        pad = pads[round_index]
+
+        def act(i, first, width, own):
+            spot = (d + i, pl.ds(side + first, width), slice(None))
+            values = x_ref[i, pl.ds(first, width), :] if own else pad[spot]
+            values = cubed(values.astype(jnp.float32))
+            half = (values - mean[None]) * half_scale[None]
+            hidden = half * jnp.tanh(half) + half
+            hidden = jnp.where(live(i, first, width), hidden, 0.0).reshape(width, channels)
+            pad[spot] = hidden.astype(jnp.bfloat16)
+
+        square = (samples, samples)
+        flag = jnp.broadcast_to(
+            flags_ref[round_index : round_index + 1, :].astype(jnp.float32), square
+        )
+        own = lax.broadcasted_iota(jnp.int32, square, 0) == lax.broadcasted_iota(
+            jnp.int32, square, 1
+        )
+        flag = jnp.where(own, flag, 0.0).sum(axis=1, keepdims=True)
+        kept = jnp.broadcast_to(flag, (samples, channels)) / KEEP_RATE
 
         def conv(first_row, height, first, width):
             taps = [
@@ -257,55 +310,69 @@
                     total = total + jnp.where(mask, values, 0.0).sum(axis=0)
                 total_ref[...] = total
 
+        edge = max(DILATIONS)
+        edge_cells = edge * samples
+        steps = tile_rows // edge
+
         def inner(step):
-            conv(step * ROWS_PER_STEP, ROWS_PER_STEP, side, cells - 2 * side)
-
-        steps = tile_rows // ROWS_PER_STEP
-        pl.loop(1, steps // 2)(inner)
-
-        @pl.when(lat > 0)
-        def _():
-            to_down.wait_recv()
-            to_up.wait_send()
-
-        @pl.when(lat < n_lat - 1)
-        def _():
-            to_up.wait_recv()
-            to_down.wait_send()
-
-        for copy in corners:
-            copy.start()
-
-        pl.loop(steps // 2, steps - 1)(inner)
-        pl.loop(0, 2)(lambda k: inner(k * (steps - 1)))
-
-        for copy in flanks + corners:
-            copy.wait()
-
-        strip_rows = 512 // side
-
-        @pl.loop(0, tile_rows // strip_rows)
-        def _(step):
-            conv(step * strip_rows, strip_rows, 0, side)
-            conv(step * strip_rows, strip_rows, cells - side, side)
+            conv(step * edge, edge, edge_cells, cells - 2 * edge_cells)
+
+        send_corners(round_index)
+
+        @pl.loop(0, tile_rows)
+        def _(i):
+            act(i, 0, cells, True)
+
+        weight_load.wait()
+        pl.loop(1, 1 + ahead)(inner)
+        wait_halos(round_index)
+
+        @pl.loop(0, tile_rows)
+        def _(i):
+            act(i, -side, side, False)
+            act(i, cells, side, False)
+
+        @pl.loop(0, 2 * d)
+        def _(k):
+            i = jnp.where(k < d, k - d, tile_rows + k - d)
+            act(i, -side, side, False)
+            act(i, 0, cells, False)
+            act(i, cells, side, False)
+
+        @pl.loop(0, 2)
+        def _(k):
+            conv(k * (tile_rows - edge), edge, 0, cells)
+
+        @pl.loop(0, 2)
+        def _(k):
+            first = pl.multiple_of(k * (cells - edge_cells), edge_cells)
+            conv(edge, tile_rows - 2 * edge, first, edge_cells)
+
+        if round_index == 0:
+            send_halos(1)
+        if ahead < steps - 2:
+            pl.loop(1 + ahead, steps - 1)(inner)
 
     total = jnp.zeros((samples, channels), jnp.float32)
     total_ref[...] = total
     for c in range(LOAD_CHUNKS):
         loads[c].wait()
         total = lax.fori_loop(c * chunk, (c + 1) * chunk, load_row, total)
+    pl.semaphore_wait(barrier, n_lat - 1 + n_lon - 1)
+    send_halos(0)
     local_statistics(0, total)
-    pl.semaphore_wait(barrier, n_lat - 1 + n_lon - 1)
-    block(0, pad1, w1_ref, loads[LOAD_CHUNKS], *global_statistics(0))
+    block(0, w1_ref, loads[LOAD_CHUNKS], 2, *global_statistics(0))
     local_statistics(1, total_ref[...])
-    block(1, pad2, w2_ref, loads[LOAD_CHUNKS + 1], *global_statistics(1))
+    last = tile_rows // max(DILATIONS) - 2
+    block(1, w2_ref, loads[LOAD_CHUNKS + 1], last, *global_statistics(1))
 
 
 def reorder(x_ref, out_ref):
     samples, rows, cols, channels = out_ref.shape
+    by_sample = permutation(samples, cols, jnp.bfloat16)
     for i in range(rows):
-        values = x_ref[i].astype(jnp.float32).reshape(cols, samples, channels)
-        out_ref[:, i] = jnp.swapaxes(values, 0, 1).astype(jnp.bfloat16)
+        values = jnp.dot(by_sample, x_ref[i], preferred_element_type=jnp.float32)
+        out_ref[:, i] = values.astype(jnp.bfloat16).reshape(samples, cols, channels)
 
 
 def per_device(n_lat, n_lon, features, band_points, survival_flags, first_weight, second_weight):
@@ -349,16 +416,16 @@
     )(
         features,
         band_points,
-        survival_flags,
+        survival_flags.T,
         first_weight.reshape(taps),
         second_weight.reshape(taps),
     )
     return pl.pallas_call(
         reorder,
-        grid=(rows // ROWS_PER_STEP,),
+        grid=(rows // REORDER_ROWS,),
         out_shape=jax.ShapeDtypeStruct(features.shape, jnp.bfloat16),
-        in_specs=[pl.BlockSpec((ROWS_PER_STEP, cols * samples, channels), lambda i: (i, 0, 0))],
-        out_specs=pl.BlockSpec((samples, ROWS_PER_STEP, cols, channels), lambda i: (0, i, 0, 0)),
+        in_specs=[pl.BlockSpec((REORDER_ROWS, cols * samples, channels), lambda i: (i, 0, 0))],
+        out_specs=pl.BlockSpec((samples, REORDER_ROWS, cols, channels), lambda i: (0, i, 0, 0)),
     )(ordered)
 
 

time: 87.5 us -> 83.9 us (0.959)
  Pallas kernels: 85.8 us -> 83.7 us
  local copies, waits for them, and re-layouts: 1.34 us -> 0 us
    pallas_call x1, Pallas kernels: 7.44 us -> 5.54 us  [per_device(): pl.pallas_call(reorder, grid=(rows // REORDER_ROWS,), out_shape=jax.Shape...]
    unnamed x1 -> x0, local copies, waits for them, and re-layouts: 1.34 us -> none
where the time goes in v2:
time: 83.9 us; the launch traced here: 83.7 us
  Pallas kernels  83.7 us (100%)
    pallas_call x1, Pallas kernels, per_device(): pl.pallas_call(functools.partial(kernel, n_lat, n_lon, rows, cols, sample...  78.2 us
    pallas_call x1, Pallas kernels, per_device(): pl.pallas_call(reorder, grid=(rows // REORDER_ROWS,), out_shape=jax.Shape...  5.54 us

profile of v2, /device:TPU:0, one launch (start us, length us, event | category | flops | bytes accessed | tf_op | source)
XLA Modules:
  0.0 83.7 jit_solution(16422582042736006068)
XLA Ops:
  0.0 78.2 %shard_map.55.x_ref = bf16[32,256,256]{2,1,0:T(8,128)(2,1)} custom-call(bf16[8,32,32,256]{3,2,1,0:T(8,128)(2,1)} %feat_hbm.1, s32[128]{0:T(128)} %points_ref.1, s32[2,8]{1,0:T(2,128)} %bitcast.5, bf16[2304,256]{1,0:T(8,128)(2,1)} %bitcast.3, bf16[2304,256]{1,0:T(8,128)(2,1)} %bitcast.4), custom_call_target="tpu_custom_call" | custom-call | tf_op jit(solution)/shard_map/pallas_call | solution.py:392
  78.2 5.5 %shard_map.56 = bf16[8,32,32,256]{3,2,1,0:T(8,128)(2,1)} custom-call(bf16[32,256,256]{2,1,0:T(8,128)(2,1)} %shard_map.55.x_ref), custom_call_target="tpu_custom_call" | custom-call | tf_op jit(solution)/shard_map/pallas_call | solution.py:423

commit v3 on v2

--- a/solution.py
+++ b/solution.py
@@ -288,16 +288,15 @@
         kept = jnp.broadcast_to(flag, (samples, channels)) / KEEP_RATE
 
         def conv(first_row, height, first, width):
-            taps = [
-                pad[
-                    pl.ds(first_row + r * d, height), pl.ds(first + c * side, width), :
-                ].reshape(height * width, channels)
-                for r in range(3)
-                for c in range(3)
-            ]
-            summed = jnp.dot(
-                jnp.concatenate(taps, axis=1), w_ref[...], preferred_element_type=jnp.float32
-            )
+            summed = None
+            for r in range(3):
+                for c in range(3):
+                    tap = pad[
+                        pl.ds(first_row + r * d, height), pl.ds(first + c * side, width), :
+                    ].reshape(height * width, channels)
+                    weight = w_ref[pl.ds((3 * r + c) * channels, channels), :]
+                    term = jnp.dot(tap, weight, preferred_element_type=jnp.float32)
+                    summed = term if summed is None else summed + term
             summed = (cubed(summed) * kept[None]).reshape(height, width, channels)
             where = (pl.ds(first_row, height), pl.ds(first, width), slice(None))
             new = (x_ref[where].astype(jnp.float32) + summed).astype(jnp.bfloat16)

time: 83.9 us -> 83.9 us (level)
  no operation moved by 1% of the time
where the time goes in v3:
time: 83.9 us; the launch traced here: 83.7 us
  Pallas kernels  83.7 us (100%)
    pallas_call x1, Pallas kernels, per_device(): pl.pallas_call(functools.partial(kernel, n_lat, n_lon, rows, cols, sample...  78.2 us
    pallas_call x1, Pallas kernels, per_device(): pl.pallas_call(reorder, grid=(rows // REORDER_ROWS,), out_shape=jax.Shape...  5.54 us

profile of v3, /device:TPU:0, one launch (start us, length us, event | category | flops | bytes accessed | tf_op | source)
XLA Modules:
  0.0 83.7 jit_solution(4050506116534117458)
XLA Ops:
  0.0 78.2 %shard_map.55.x_ref = bf16[32,256,256]{2,1,0:T(8,128)(2,1)} custom-call(bf16[8,32,32,256]{3,2,1,0:T(8,128)(2,1)} %feat_hbm.1, s32[128]{0:T(128)} %points_ref.1, s32[2,8]{1,0:T(2,128)} %bitcast.5, bf16[2304,256]{1,0:T(8,128)(2,1)} %bitcast.3, bf16[2304,256]{1,0:T(8,128)(2,1)} %bitcast.4), custom_call_target="tpu_custom_call" | custom-call | tf_op jit(solution)/shard_map/pallas_call | solution.py:391
  78.2 5.5 %shard_map.56 = bf16[8,32,32,256]{3,2,1,0:T(8,128)(2,1)} custom-call(bf16[32,256,256]{2,1,0:T(8,128)(2,1)} %shard_map.55.x_ref), custom_call_target="tpu_custom_call" | custom-call | tf_op jit(solution)/shard_map/pallas_call | solution.py:422
